TPU v7x, 256 devices: a whole 4x4x8 slice. The times are simulated.
256 devices in a mesh: leaf: 16 (over z, core), front: 16 (over x, y).
Axes of the slice: x: 4, y: 4, z: 8, core: 2. Of those that a mesh axis runs over, the one named last changes fastest.
Arguments:
- right_side_0: bfloat16 [16, 16, 256, 128], P('leaf', 'front'), may hold values from -6 to 6
- right_side_1: bfloat16 [16, 16, 128, 128], P('leaf', 'front'), may hold values from -6 to 6
- right_side_2: bfloat16 [16, 16, 64, 128], P('leaf', 'front'), may hold values from -6 to 6
- right_side_3: bfloat16 [16, 16, 32, 128], P('leaf', 'front'), may hold values from -6 to 6
- right_side_4: bfloat16 [16, 16, 16, 128], P('leaf', 'front'), may hold values from -6 to 6
- inverse_0: bfloat16 [16, 16, 256, 4096], P('leaf', 'front'), as said below
- inverse_1: bfloat16 [16, 16, 128, 4096], P('leaf', 'front'), as said below
- inverse_2: bfloat16 [16, 16, 64, 4096], P('leaf', 'front'), as said below
- inverse_3: bfloat16 [16, 16, 32, 4096], P('leaf', 'front'), as said below
- inverse_4: bfloat16 [16, 16, 16, 4096], P('leaf', 'front'), as said below
- lower_0: bfloat16 [16, 16, 256, 2048], P('leaf', 'front'), may hold values from -0.0625 to 0.0625
- lower_1: bfloat16 [16, 16, 128, 2048], P('leaf', 'front'), may hold values from -0.0625 to 0.0625
- lower_2: bfloat16 [16, 16, 64, 2048], P('leaf', 'front'), may hold values from -0.0625 to 0.0625
- lower_3: bfloat16 [16, 16, 32, 2048], P('leaf', 'front'), may hold values from -0.0625 to 0.0625
- block_map_0: int32 [16, 16], replicated, may hold values from 0 to 47, as said below
- block_map_1: int32 [8, 16], replicated, may hold values from 0 to 47, as said below
- block_map_2: int32 [4, 16], replicated, may hold values from 0 to 47, as said below
- block_map_3: int32 [2, 16], replicated, may hold values from 0 to 31, as said below
Outputs:
- solution_0: float32 [16, 16, 256, 128], P('leaf', 'front')
- solution_1: float32 [16, 16, 128, 128], P('leaf', 'front')
- solution_2: float32 [16, 16, 64, 128], P('leaf', 'front')
- solution_3: float32 [16, 16, 32, 128], P('leaf', 'front')
- solution_4: float32 [16, 16, 16, 128], P('leaf', 'front')
Inputs may be any that keep to these rules, and one draw needn't show every extreme that they name: `inverse_0`: each front's pivot inverse is lower triangular, with its diagonal between 0.8 and 1.2. `inverse_1`: as for inverse_0. `inverse_2`: as for inverse_0. `inverse_3`: as for inverse_0. `inverse_4`: as for inverse_0. `block_map_0`: each row's entries are all different and increasing; the last entry of every row is the parent's last block. `block_map_1`: as for block_map_0. `block_map_2`: as for block_map_0. `block_map_3`: as for block_map_0, into the root's pivot blocks.
All inputs are finite; a program needn't handle non-finite values.
Results may differ from a plain program's by a relative error of at most 0.033.
Values may be sent and summed in bfloat16 or wider, within the bound.
A program may use at most 128 MiB of HBM per device.

v0:
```python
import jax
import jax.numpy as jnp
from jax import lax
from jax.sharding import PartitionSpec as P

BLOCK = 128
CELLS = 16


def swapped(value, axis, stride):
    mask = 2**stride
    pairs = [(source, source ^ mask) for source in range(lax.axis_size(axis))]
    return lax.ppermute(value, axis, pairs)


def group_gather(pieces, slab_count):
    local_count = pieces.shape[0]
    gathered = lax.all_gather(pieces, "front", axis=1, tiled=True)
    group_span = max(1, slab_count // local_count)
    leaf_index = lax.axis_index("leaf")
    for level_bit in range(group_span.bit_length() - 1):
        partner = swapped(gathered, "leaf", level_bit)
        upper_side = leaf_index >> level_bit & 1 == 1
        gathered = jnp.where(
            upper_side,
            jnp.concatenate([partner, gathered], 0),
            jnp.concatenate([gathered, partner], 0),
        )
    front_count = max(1, local_count // slab_count)
    return gathered.reshape(front_count, -1, gathered.shape[-1])


def group_share(partial_value, slab_count, cell_count, local_count):
    width = partial_value.shape[-1]
    grid = partial_value.reshape(-1, CELLS, cell_count, width)
    group_span = max(1, slab_count // local_count)
    leaf_index = lax.axis_index("leaf")
    for level_bit in reversed(range(group_span.bit_length() - 1)):
        middle = grid.shape[0] // 2
        lower_half = grid[:middle]
        upper_half = grid[middle:]
        upper_side = leaf_index >> level_bit & 1 == 1
        keeping = jnp.where(upper_side, upper_half, lower_half)
        sending = jnp.where(upper_side, lower_half, upper_half)
        grid = keeping + swapped(sending.astype(jnp.bfloat16), "leaf", level_bit).astype(
            sending.dtype
        )
    return lax.psum_scatter(
        grid.astype(jnp.bfloat16), "front", scatter_dimension=1, tiled=True
    ).astype(jnp.float32)


def own_cells(full, slab_count, cell_count, local_count, front_local):
    grid = full.reshape(-1, CELLS, cell_count, full.shape[-1])
    group_span = max(1, slab_count // local_count)
    offset = lax.axis_index("leaf") % group_span * local_count
    grid = lax.dynamic_slice_in_dim(grid, offset, local_count, 0)
    return lax.dynamic_slice_in_dim(grid, lax.axis_index("front") * front_local, front_local, 1)


def assemble(stacked, block_map, first_parent, blocks_total):
    parent_count = stacked.shape[0]
    width = stacked.shape[-1]
    chosen = lax.dynamic_slice_in_dim(block_map, 2 * first_parent, 2 * parent_count, 0)
    chosen = chosen.reshape(parent_count, -1)
    targets = lax.broadcasted_iota(jnp.int32, (parent_count, blocks_total, chosen.shape[1]), 1)
    selector = (targets == chosen[:, None, :]).astype(jnp.bfloat16)
    blocks = stacked.reshape(parent_count, chosen.shape[1], BLOCK, width)
    summed = jnp.einsum("fpj,fjbr->fpbr", selector, blocks, preferred_element_type=jnp.float32)
    return summed.reshape(parent_count, blocks_total * BLOCK, width)


def pick_blocks(table, where):
    return table[where]


def solve(right_sides, inverses, lowers, block_maps):
    local_count = inverses[0].shape[0]
    front_local = inverses[0].shape[1]
    pivots = inverses[0].shape[-1]
    contribution = lowers[0].shape[-1]
    width = right_sides[0].shape[-1]
    leaf_index = lax.axis_index("leaf")
    upward = []
    assembled = None
    for height in range(5):
        slab_count = 2**height
        front_count = max(1, local_count // slab_count)
        cell_count = inverses[height].shape[2]
        if height == 0:
            pivot_part = jnp.zeros((front_count, pivots, width), jnp.float32)
        else:
            pivot_part = assembled[:, :pivots]
        own_part = own_cells(pivot_part, slab_count, cell_count, local_count, front_local)
        mine = (right_sides[height].astype(jnp.float32) - own_part).astype(jnp.bfloat16)
        right = group_gather(mine, slab_count)
        factor = inverses[height].reshape(front_count, -1, pivots)
        solved = jnp.einsum(
            "fmp,fpr->fmr", factor, right, preferred_element_type=jnp.float32
        ).astype(jnp.bfloat16)
        upward.append(solved)
        if height < 4:
            coupling = lowers[height].reshape(front_count, -1, contribution)
            partial_value = jnp.einsum(
                "fmc,fmr->fcr", coupling, solved, preferred_element_type=jnp.float32
            )
            update_rows = contribution // (CELLS * slab_count)
            update_cells = group_share(partial_value, slab_count, update_rows, local_count)
            if height > 0:
                update_cells = update_cells + own_cells(
                    assembled[:, pivots:], slab_count, update_rows, local_count, front_local
                )
            update_cells = update_cells.astype(jnp.bfloat16)
            stacked = group_gather(update_cells, 2 * slab_count)
            first_parent = leaf_index * local_count // (2 * slab_count)
            blocks_total = (pivots + contribution) // BLOCK if height < 3 else pivots // BLOCK
            assembled = assemble(stacked, block_maps[height], first_parent, blocks_total)
    solutions = [None] * 5
    parent = None
    gathered = None
    for height in (4, 3, 2, 1, 0):
        slab_count = 2**height
        front_count = max(1, local_count // slab_count)
        cell_count = inverses[height].shape[2]
        factor = inverses[height].reshape(front_count, -1, pivots)
        if height == 4:
            adjusted = upward[4]
        else:
            first_front = leaf_index * local_count // slab_count
            chosen = lax.dynamic_slice_in_dim(block_maps[height], first_front, front_count, 0)
            expanded = jnp.repeat(parent, 2, axis=0)[:front_count]
            blocks = expanded.reshape(front_count, -1, BLOCK, width)
            gathered = jax.vmap(pick_blocks)(blocks, chosen).reshape(
                front_count, contribution, width
            )
            coupling = lowers[height].reshape(front_count, -1, contribution)
            reaction = jnp.einsum(
                "fmc,fcr->fmr", coupling, gathered, preferred_element_type=jnp.float32
            )
            adjusted = (upward[height].astype(jnp.float32) - reaction).astype(jnp.bfloat16)
        partial_value = jnp.einsum(
            "fmp,fmr->fpr", factor, adjusted, preferred_element_type=jnp.float32
        )
        solution = group_share(partial_value, slab_count, cell_count, local_count)
        solutions[height] = solution
        if height > 0:
            rounded = group_gather(solution.astype(jnp.bfloat16), slab_count)
            parent = rounded if height == 4 else jnp.concatenate([rounded, gathered], 1)
    return solutions


def on_device(
    right_side_0,
    right_side_1,
    right_side_2,
    right_side_3,
    right_side_4,
    inverse_0,
    inverse_1,
    inverse_2,
    inverse_3,
    inverse_4,
    lower_0,
    lower_1,
    lower_2,
    lower_3,
    block_map_0,
    block_map_1,
    block_map_2,
    block_map_3,
):
    right_sides = [right_side_0, right_side_1, right_side_2, right_side_3, right_side_4]
    inverses = [inverse_0, inverse_1, inverse_2, inverse_3, inverse_4]
    lowers = [lower_0, lower_1, lower_2, lower_3]
    block_maps = [block_map_0, block_map_1, block_map_2, block_map_3]
    joined = solve(right_sides, inverses, lowers, block_maps)
    return (joined[0], joined[1], joined[2], joined[3], joined[4])


def solution(mesh):
    return jax.shard_map(
        on_device,
        mesh=mesh,
        in_specs=(
            P("leaf", "front", None, None),
            P("leaf", "front", None, None),
            P("leaf", "front", None, None),
            P("leaf", "front", None, None),
            P("leaf", "front", None, None),
            P("leaf", "front", None, None),
            P("leaf", "front", None, None),
            P("leaf", "front", None, None),
            P("leaf", "front", None, None),
            P("leaf", "front", None, None),
            P("leaf", "front", None, None),
            P("leaf", "front", None, None),
            P("leaf", "front", None, None),
            P("leaf", "front", None, None),
            P(),
            P(),
            P(),
            P(),
        ),
        out_specs=(
            P("leaf", "front", None, None),
            P("leaf", "front", None, None),
            P("leaf", "front", None, None),
            P("leaf", "front", None, None),
            P("leaf", "front", None, None),
        ),
        check_vma=False,
    )
```

profile of v0, /device:TPU:1, one launch (start us, length us, event | category | flops | bytes accessed | tf_op | source)
XLA Modules:
  0.0 1559.6 jit_solution(12473457194144096916)
XLA Ops:
  10.3 50.3 %all-gather.2.cloned.1.call-done = bf16[1,16,256,128]{3,2,0,1:T(8,128)(2,1)} async-done(((bf16[1,1,256,128]{3,2,0,1:T(8,128)(2,1)}), bf16[1,16,256,128]{3,2,0,1:T(8,128)(2,1)}) %all-gather.2.cloned.1.call-update) | async-done | bytes 1048592 | tf_op jit(solution)/shard_map/all_gather | solution.py:18
  64.0 76.5 %reduce-scatter.49.cloned.1.call-done = bf16[1,1,128,128]{2,3,1,0:T(8,128)(2,1)} async-done(((bf16[1,16,128,128]{2,3,1,0:T(8,128)(2,1)}), bf16[1,1,128,128]{2,3,1,0:T(8,128)(2,1)}) %reduce-scatter.49.cloned.1.call-update) | async-done | bytes 32784
  141.4 17.5 %all_gather.40 = bf16[1,16,128,128]{3,2,0,1:T(8,128)(2,1)S(1)} all-gather(bf16[1,1,128,128]{3,2,0,1:T(8,128)(2,1)S(1)} %copy.134), channel_id=1, replica_groups=mesh['leaf'=16,'front'=16] {'front'}, dimensions={1}, use_global_device_ids=true | all-gather | bytes 557056 | tf_op jit(solution)/shard_map/all_gather | solution.py:18
  158.9 8.1 collective-permute-start
  172.2 16.5 %all_gather.41 = bf16[1,16,128,128]{3,2,0,1:T(8,128)(2,1)S(1)} all-gather(bf16[1,1,128,128]{3,2,0,1:T(8,128)(2,1)S(1)} %fusion.44), channel_id=1, replica_groups=mesh['leaf'=16,'front'=16] {'front'}, dimensions={1}, use_global_device_ids=true | all-gather | bytes 557056 | tf_op jit(solution)/shard_map/all_gather | solution.py:18
  201.0 73.2 %reduce-scatter.51.cloned.1.call-done = bf16[1,1,64,128]{3,2,1,0:T(8,128)(2,1)} async-done(((bf16[1,16,64,128]{3,2,1,0:T(8,128)(2,1)}), bf16[1,1,64,128]{3,2,1,0:T(8,128)(2,1)}) %reduce-scatter.51.cloned.1.call-update) | async-done | bytes 16400
  274.9 17.0 %all_gather.42 = bf16[1,16,64,128]{3,2,0,1:T(8,128)(2,1)S(1)} all-gather(bf16[1,1,64,128]{3,2,0,1:T(8,128)(2,1)S(1)} %fusion.47), channel_id=1, replica_groups=mesh['leaf'=16,'front'=16] {'front'}, dimensions={1}, use_global_device_ids=true | all-gather | bytes 278528 | tf_op jit(solution)/shard_map/all_gather | solution.py:18
  291.9 8.4 collective-permute-start.3
  303.7 11.1 collective-permute-done.4
  318.5 16.3 %all_gather.43 = bf16[1,16,64,128]{3,2,0,1:T(8,128)(2,1)S(1)} all-gather(bf16[1,1,64,128]{3,2,0,1:T(8,128)(2,1)S(1)} %fusion.45), channel_id=1, replica_groups=mesh['leaf'=16,'front'=16] {'front'}, dimensions={1}, use_global_device_ids=true | all-gather | bytes 278528 | tf_op jit(solution)/shard_map/all_gather | solution.py:18
  344.4 11.9 collective-permute-done.6
  369.4 72.8 %reduce-scatter.53.cloned.1.call-done = bf16[1,1,32,128]{3,2,1,0:T(8,128)(2,1)} async-done(((bf16[1,16,32,128]{3,2,1,0:T(8,128)(2,1)}), bf16[1,1,32,128]{3,2,1,0:T(8,128)(2,1)}) %reduce-scatter.53.cloned.1.call-update) | async-done | bytes 8208
  443.0 17.2 %all_gather.44 = bf16[1,16,32,128]{3,2,0,1:T(8,128)(2,1)S(1)} all-gather(bf16[1,1,32,128]{3,2,0,1:T(8,128)(2,1)S(1)} %fusion.58), channel_id=1, replica_groups=mesh['leaf'=16,'front'=16] {'front'}, dimensions={1}, use_global_device_ids=true | all-gather | bytes 139264 | tf_op jit(solution)/shard_map/all_gather | solution.py:18
  460.1 8.5 collective-permute-start.9
  479.8 22.5 %collective-permute-done.11 = bf16[4,16,32,128]{3,2,1,0:T(8,128)(2,1)S(1)} collective-permute-done((bf16[4,16,32,128]{3,2,1,0:T(8,128)(2,1)S(1)}, bf16[4,16,32,128]{3,2,1,0:T(8,128)(2,1)S(1)}, u32[]{:S(2)}, u32[]{:S(2)}) %collective-permute-start.11) | collective-permute-done | bytes 524320 | tf_op jit(solution)/shard_map/ppermute | solution.py:13
  506.0 16.4 %all_gather.45 = bf16[1,16,32,128]{3,2,0,1:T(8,128)(2,1)S(1)} all-gather(bf16[1,1,32,128]{3,2,0,1:T(8,128)(2,1)S(1)} %fusion.48), channel_id=1, replica_groups=mesh['leaf'=16,'front'=16] {'front'}, dimensions={1}, use_global_device_ids=true | all-gather | bytes 139264 | tf_op jit(solution)/shard_map/all_gather | solution.py:18
  530.7 7.2 collective-permute-done.13
  540.3 22.9 %collective-permute-done.14 = bf16[4,16,32,128]{3,2,1,0:T(8,128)(2,1)S(1)} collective-permute-done((bf16[4,16,32,128]{3,2,1,0:T(8,128)(2,1)S(1)}, bf16[4,16,32,128]{3,2,1,0:T(8,128)(2,1)S(1)}, u32[]{:S(2)}, u32[]{:S(2)}) %collective-permute-start.14) | collective-permute-done | bytes 524320 | tf_op jit(solution)/shard_map/ppermute | solution.py:13
  564.6 12.9 collective-permute-done.15
  588.6 85.7 %all-reduce.12.cloned.1.call-done = bf16[1,16,16,128]{3,2,1,0:T(8,128)(2,1)} async-done(((bf16[1,16,16,128]{3,2,1,0:T(8,128)(2,1)}), bf16[1,16,16,128]{3,2,1,0:T(8,128)(2,1)}) %all-reduce.12.cloned.1.call-update) | async-done | bytes 65552
  675.7 17.5 %all_gather.46 = bf16[1,16,16,128]{3,2,0,1:T(8,128)(2,1)S(1)} all-gather(bf16[1,1,16,128]{3,2,0,1:T(8,128)(2,1)S(1)} %fusion.63), channel_id=1, replica_groups=mesh['leaf'=16,'front'=16] {'front'}, dimensions={1}, use_global_device_ids=true | all-gather | bytes 69632 | tf_op jit(solution)/shard_map/all_gather | solution.py:18
  693.1 7.8 collective-permute-start.18
  709.0 11.4 collective-permute-done.20
  727.1 22.8 %collective-permute-done.21 = bf16[8,16,16,128]{3,2,1,0:T(8,128)(2,1)S(1)} collective-permute-done((bf16[8,16,16,128]{3,2,1,0:T(8,128)(2,1)S(1)}, bf16[8,16,16,128]{3,2,1,0:T(8,128)(2,1)S(1)}, u32[]{:S(2)}, u32[]{:S(2)}) %collective-permute-start.21) | collective-permute-done | bytes 524320 | tf_op jit(solution)/shard_map/ppermute | solution.py:13
  752.0 16.1 %all_gather.47 = bf16[1,16,16,128]{3,2,0,1:T(8,128)(2,1)S(1)} all-gather(bf16[1,1,16,128]{3,2,0,1:T(8,128)(2,1)S(1)} %fusion.64), channel_id=1, replica_groups=mesh['leaf'=16,'front'=16] {'front'}, dimensions={1}, use_global_device_ids=true | all-gather | bytes 69632 | tf_op jit(solution)/shard_map/all_gather | solution.py:18
  781.8 13.7 collective-permute-done.24
  798.3 25.9 %collective-permute-done.25 = bf16[8,16,16,128]{3,2,1,0:T(8,128)(2,1)S(1)} collective-permute-done((bf16[8,16,16,128]{3,2,1,0:T(8,128)(2,1)S(1)}, bf16[8,16,16,128]{3,2,1,0:T(8,128)(2,1)S(1)}, u32[]{:S(2)}, u32[]{:S(2)}) %collective-permute-start.25) | collective-permute-done | bytes 524320 | tf_op jit(solution)/shard_map/ppermute | solution.py:13
  835.7 13.4 collective-permute-done.26
  850.5 13.8 collective-permute-done.27
  872.1 86.2 %all-reduce.14.cloned.1.call-done = bf16[1,16,16,128]{3,2,1,0:T(8,128)(2,1)} async-done(((bf16[1,16,16,128]{3,2,1,0:T(8,128)(2,1)}), bf16[1,16,16,128]{3,2,1,0:T(8,128)(2,1)}) %all-reduce.14.cloned.1.call-update) | async-done | bytes 65552
  960.2 17.7 %all_gather.48 = bf16[1,16,16,128]{3,2,0,1:T(8,128)(2,1)S(1)} all-gather(bf16[1,1,16,128]{3,2,0,1:T(8,128)(2,1)S(1)} %get-tuple-element.26), channel_id=1, replica_groups=mesh['leaf'=16,'front'=16] {'front'}, dimensions={1}, use_global_device_ids=true | all-gather | bytes 69632 | tf_op jit(solution)/shard_map/all_gather | solution.py:18
  977.9 7.8 collective-permute-start.30
  993.8 11.4 collective-permute-done.32
  1011.8 22.8 %collective-permute-done.33 = bf16[8,16,16,128]{3,2,1,0:T(8,128)(2,1)S(1)} collective-permute-done((bf16[8,16,16,128]{3,2,1,0:T(8,128)(2,1)S(1)}, bf16[8,16,16,128]{3,2,1,0:T(8,128)(2,1)S(1)}, u32[]{:S(2)}, u32[]{:S(2)}) %collective-permute-start.33) | collective-permute-done | bytes 524320 | tf_op jit(solution)/shard_map/ppermute | solution.py:13
  1043.7 23.1 %collective-permute-done.34 = bf16[4,16,32,128]{3,2,1,0:T(8,128)(2,1)} collective-permute-done((bf16[4,16,32,128]{3,2,1,0:T(8,128)(2,1)}, bf16[4,16,32,128]{3,2,1,0:T(8,128)(2,1)}, u32[]{:S(2)}, u32[]{:S(2)}) %collective-permute-start.34) | collective-permute-done | bytes 524320 | tf_op jit(solution)/shard_map/ppermute | solution.py:13
  1078.9 69.8 %reduce-scatter.55.cloned.1.call-done = bf16[1,1,32,128]{3,2,1,0:T(8,128)(2,1)} async-done(((bf16[1,16,32,128]{3,2,1,0:T(8,128)(2,1)}), bf16[1,1,32,128]{3,2,1,0:T(8,128)(2,1)}) %reduce-scatter.55.cloned.1.call-update) | async-done | bytes 8208
  1148.7 17.2 %all_gather.49 = bf16[1,16,32,128]{3,2,0,1:T(8,128)(2,1)S(1)} all-gather(bf16[1,1,32,128]{3,2,0,1:T(8,128)(2,1)} %bitcast.395), channel_id=1, replica_groups=mesh['leaf'=16,'front'=16] {'front'}, dimensions={1}, use_global_device_ids=true | all-gather | bytes 139264 | tf_op jit(solution)/shard_map/all_gather | solution.py:18
  1165.9 8.5 collective-permute-start.37
  1185.5 22.6 %collective-permute-done.39 = bf16[4,16,32,128]{3,2,1,0:T(8,128)(2,1)S(1)} collective-permute-done((bf16[4,16,32,128]{3,2,1,0:T(8,128)(2,1)S(1)}, bf16[4,16,32,128]{3,2,1,0:T(8,128)(2,1)S(1)}, u32[]{:S(2)}, u32[]{:S(2)}) %collective-permute-start.39) | collective-permute-done | bytes 524320 | tf_op jit(solution)/shard_map/ppermute | solution.py:13
  1218.7 8.4 collective-permute-done.40
  1232.7 74.9 %reduce-scatter.57.cloned.1.call-done = bf16[1,1,64,128]{3,2,1,0:T(8,128)(2,1)} async-done(((bf16[1,16,64,128]{3,2,1,0:T(8,128)(2,1)}), bf16[1,1,64,128]{3,2,1,0:T(8,128)(2,1)}) %reduce-scatter.57.cloned.1.call-update) | async-done | bytes 16400
  1307.6 17.0 %all_gather.50 = bf16[1,16,64,128]{3,2,0,1:T(8,128)(2,1)S(1)} all-gather(bf16[1,1,64,128]{3,2,0,1:T(8,128)(2,1)} %bitcast.393), channel_id=1, replica_groups=mesh['leaf'=16,'front'=16] {'front'}, dimensions={1}, use_global_device_ids=true | all-gather | bytes 278528 | tf_op jit(solution)/shard_map/all_gather | solution.py:18
  1324.6 8.7 collective-permute-start.42
  1337.4 10.4 collective-permute-done.43
  1360.8 74.0 %reduce-scatter.59.cloned.1.call-done = bf16[1,1,128,128]{2,3,1,0:T(8,128)(2,1)} async-done(((bf16[1,16,128,128]{2,3,1,0:T(8,128)(2,1)}), bf16[1,1,128,128]{2,3,1,0:T(8,128)(2,1)}) %reduce-scatter.59.cloned.1.call-update) | async-done | bytes 32784
  1435.7 19.8 %all_gather.51 = bf16[1,16,128,128]{3,2,0,1:T(8,128)(2,1)} all-gather(bf16[1,1,128,128]{3,2,0,1:T(8,128)(2,1)S(1)} %copy.203), channel_id=1, replica_groups=mesh['leaf'=16,'front'=16] {'front'}, dimensions={1}, use_global_device_ids=true | all-gather | bytes 557056 | tf_op jit(solution)/shard_map/all_gather | solution.py:18
  1455.5 7.8 collective-permute-start.45
  1478.1 72.6 %reduce-scatter.61.cloned.1.call-done = bf16[1,1,256,128]{2,3,1,0:T(8,128)(2,1)} async-done(((bf16[1,16,256,128]{2,3,1,0:T(8,128)(2,1)}), bf16[1,1,256,128]{2,3,1,0:T(8,128)(2,1)}) %reduce-scatter.61.cloned.1.call-update) | async-done | bytes 65552
  (288 shorter events, 247.9 us)
Async XLA Ops:
  7.2 53.4 %all-gather.2.cloned.1.call-start = ((), (), s32[]{:S(2)}) async-start(), calls=%async_computation.7 | async-start | bytes 1114112 | tf_op jit(solution)/shard_map/all_gather | solution.py:18
  7.9 132.6 %reduce-scatter.49.cloned.1.call-start = ((), (), s32[]{:S(2)}) async-start(), calls=%async_computation.10 | async-start | bytes 557056
  64.0 210.2 %reduce-scatter.51.cloned.1.call-start = ((), (), s32[]{:S(2)}) async-start(), calls=%async_computation.11 | async-start | bytes 278528
  158.9 9.7 collective-permute-start
  188.7 7.3 collective-permute-start.1
  199.7 242.6 %reduce-scatter.53.cloned.1.call-start = ((), (), s32[]{:S(2)}) async-start(), calls=%async_computation.12 | async-start | bytes 139264
  291.9 9.6 collective-permute-start.3
  301.6 13.2 collective-permute-start.4
  334.9 8.1 collective-permute-start.5
  343.1 13.2 collective-permute-start.6
  357.3 6.7 collective-permute-start.7
  368.1 306.3 %all-reduce.12.cloned.1.call-start = ((), (), s32[]{:S(2)}) async-start(), calls=%async_computation.8 | async-start | bytes 131072
  460.1 9.4 collective-permute-start.9
  469.6 7.6 collective-permute-start.10
  477.3 25.0 %collective-permute-start.11 = (bf16[4,16,32,128]{3,2,1,0:T(8,128)(2,1)S(1)}, bf16[4,16,32,128]{3,2,1,0:T(8,128)(2,1)S(1)}, u32[]{:S(2)}, u32[]{:S(2)}) collective-permute-start(bf16[4,16,32,128]{3,2,1,0:T(8,128)(2,1)S(1)} %maximum_select_fusion.14), channel_id=1, source_target_pairs={{0,64},{16,80},{32,96},{48,112},{64,0},{80,16},{96,32},{112,48},{1... | collective-permute-start | bytes 1572872 | tf_op jit(solution)/shard_map/ppermute | solution.py:13
  522.4 7.8 collective-permute-start.12
  530.3 7.6 collective-permute-start.13
  538.0 25.2 %collective-permute-start.14 = (bf16[4,16,32,128]{3,2,1,0:T(8,128)(2,1)S(1)}, bf16[4,16,32,128]{3,2,1,0:T(8,128)(2,1)S(1)}, u32[]{:S(2)}, u32[]{:S(2)}) collective-permute-start(bf16[4,16,32,128]{3,2,1,0:T(8,128)(2,1)S(1)} %maximum_select_fusion.15), channel_id=1, source_target_pairs={{0,64},{16,80},{32,96},{48,112},{64,0},{80,16},{96,32},{112,48},{1... | collective-permute-start | bytes 1572872 | tf_op jit(solution)/shard_map/ppermute | solution.py:13
  564.3 13.2 collective-permute-start.15
  586.6 371.7 %all-reduce.14.cloned.1.call-start = ((), (), s32[]{:S(2)}) async-start(), calls=%async_computation.9 | async-start | bytes 131072
  693.1 8.7 collective-permute-start.18
  701.8 4.8 collective-permute-start.19
  706.6 13.8 collective-permute-start.20
  720.5 29.4 %collective-permute-start.21 = (bf16[8,16,16,128]{3,2,1,0:T(8,128)(2,1)S(1)}, bf16[8,16,16,128]{3,2,1,0:T(8,128)(2,1)S(1)}, u32[]{:S(2)}, u32[]{:S(2)}) collective-permute-start(bf16[8,16,16,128]{3,2,1,0:T(8,128)(2,1)S(1)} %maximum_select_fusion.16), channel_id=1, source_target_pairs={{0,128},{16,144},{32,160},{48,176},{64,192},{80,208},{96,224},{112... | collective-permute-start | bytes 1572872 | tf_op jit(solution)/shard_map/ppermute | solution.py:13
  768.1 7.7 collective-permute-start.22
  775.9 4.8 collective-permute-start.23
  780.7 14.8 collective-permute-start.24
  795.6 28.6 %collective-permute-start.25 = (bf16[8,16,16,128]{3,2,1,0:T(8,128)(2,1)S(1)}, bf16[8,16,16,128]{3,2,1,0:T(8,128)(2,1)S(1)}, u32[]{:S(2)}, u32[]{:S(2)}) collective-permute-start(bf16[8,16,16,128]{3,2,1,0:T(8,128)(2,1)S(1)} %maximum_select_fusion.17), channel_id=1, source_target_pairs={{0,128},{16,144},{32,160},{48,176},{64,192},{80,208},{96,224},{112... | collective-permute-start | bytes 1572872 | tf_op jit(solution)/shard_map/ppermute | solution.py:13
  830.3 18.9 %collective-permute-start.26 = (bf16[8,16,16,128]{3,2,1,0:T(8,128)(2,1)}, bf16[8,16,16,128]{3,2,1,0:T(8,128)(2,1)}, u32[]{:S(2)}, u32[]{:S(2)}) collective-permute-start(bf16[8,16,16,128]{3,2,1,0:T(8,128)(2,1)} %bitcast.380), channel_id=1, source_target_pairs={{0,128},{16,144},{32,160},{48,176},{64,192},{80,208},{96,224},{112... | collective-permute-start | bytes 1572872 | tf_op jit(solution)/shard_map/ppermute | solution.py:13
  850.4 13.9 collective-permute-start.27
  864.3 4.7 collective-permute-start.28
  872.1 276.6 %reduce-scatter.55.cloned.1.call-start = ((), (), s32[]{:S(2)}) async-start(), calls=%async_computation.13 | async-start | bytes 139264
  977.9 8.7 collective-permute-start.30
  986.6 4.8 collective-permute-start.31
  991.4 13.8 collective-permute-start.32
  1005.3 29.4 %collective-permute-start.33 = (bf16[8,16,16,128]{3,2,1,0:T(8,128)(2,1)S(1)}, bf16[8,16,16,128]{3,2,1,0:T(8,128)(2,1)S(1)}, u32[]{:S(2)}, u32[]{:S(2)}) collective-permute-start(bf16[8,16,16,128]{3,2,1,0:T(8,128)(2,1)S(1)} %maximum_select_fusion.18), channel_id=1, source_target_pairs={{0,128},{16,144},{32,160},{48,176},{64,192},{80,208},{96,224},{112... | collective-permute-start | bytes 1572872 | tf_op jit(solution)/shard_map/ppermute | solution.py:13
  1041.0 25.8 %collective-permute-start.34 = (bf16[4,16,32,128]{3,2,1,0:T(8,128)(2,1)}, bf16[4,16,32,128]{3,2,1,0:T(8,128)(2,1)}, u32[]{:S(2)}, u32[]{:S(2)}) collective-permute-start(bf16[4,16,32,128]{3,2,1,0:T(8,128)(2,1)} %bitcast.381), channel_id=1, source_target_pairs={{0,64},{16,80},{32,96},{48,112},{64,0},{80,16},{96,32},{112,48},{1... | collective-permute-start | bytes 1572872 | tf_op jit(solution)/shard_map/ppermute | solution.py:13
  1068.1 6.9 collective-permute-start.35
  1078.9 228.8 %reduce-scatter.57.cloned.1.call-start = ((), (), s32[]{:S(2)}) async-start(), calls=%async_computation.14 | async-start | bytes 278528
  1165.9 9.4 collective-permute-start.37
  1175.4 7.6 collective-permute-start.38
  1183.1 25.0 %collective-permute-start.39 = (bf16[4,16,32,128]{3,2,1,0:T(8,128)(2,1)S(1)}, bf16[4,16,32,128]{3,2,1,0:T(8,128)(2,1)S(1)}, u32[]{:S(2)}, u32[]{:S(2)}) collective-permute-start(bf16[4,16,32,128]{3,2,1,0:T(8,128)(2,1)S(1)} %maximum_select_fusion.19), channel_id=1, source_target_pairs={{0,64},{16,80},{32,96},{48,112},{64,0},{80,16},{96,32},{112,48},{1... | collective-permute-start | bytes 1572872 | tf_op jit(solution)/shard_map/ppermute | solution.py:13
  1214.7 12.5 collective-permute-start.40
  1232.7 202.2 %reduce-scatter.59.cloned.1.call-start = ((), (), s32[]{:S(2)}) async-start(), calls=%async_computation.15 | async-start | bytes 557056
  1324.6 9.9 collective-permute-start.42
  1334.6 13.2 collective-permute-start.43
  1360.8 190.0 %reduce-scatter.61.cloned.1.call-start = ((), (), s32[]{:S(2)}) async-start(), calls=%async_computation.16 | async-start | bytes 1114112
  1455.5 11.1 collective-permute-start.45
  (33 other events, 966.9 us)
Sparse Core Ops, SparseCore 0:
  10.5 50.0 all-gather.1
  64.1 76.3 reduce-scatter.48
  199.8 74.3 reduce-scatter.50
  368.2 74.0 reduce-scatter.52
  586.8 87.5 all-reduce.11
  872.2 86.0 all-reduce.13
  1079.0 69.6 reduce-scatter.54
  1232.8 74.7 reduce-scatter.56
  1360.9 73.9 reduce-scatter.58
  1476.3 74.4 reduce-scatter.60
where the time goes:
time: 1570 us; the launch traced here: 1560 us
  waiting for transfers between devices  1090 us (69%)
  blocking collectives  206 us (13%)
  starting transfers between devices  150 us (10%)
  local copies, waits for them, and re-layouts  48.6 us (3%)
  other arithmetic  32.6 us (2%)
  matrix products  20 us (1%)
    unnamed x19, waiting for transfers between devices  687 us
    ppermute x46, waiting for transfers between devices, swapped(): return lax.ppermute(value, axis, pairs)  350 us
    all_gather x12, blocking collectives, group_gather(): gathered = lax.all_gather(pieces, 'front', axis=1, tiled=True)  206 us
    ppermute x46, starting transfers between devices, swapped(): return lax.ppermute(value, axis, pairs)  149 us
    all_gather x1, waiting for transfers between devices, group_gather(): gathered = lax.all_gather(pieces, 'front', axis=1, tiled=True)  50.3 us
  transfers between devices with their start and end apart: 56, of which 54 were waited for; matrix products, arithmetic and copies ran while one was open for 2% of the time, Pallas kernels for 0%

commit v1 on v0

v1 whole, which is shorter than its diff:
```python
import types

import jax
import jax.numpy as jnp
from jax import lax
from jax.experimental import pallas as pl
from jax.experimental.pallas import tpu as pltpu
from jax.sharding import PartitionSpec as P

MESH = pl.DeviceIdType.MESH
BF = jnp.bfloat16
F32 = jnp.float32
NT = (((1,), (1,)), ((), ()))
NN = (((1,), (0,)), ((), ()))
FRONT = 16
LEVELS = range(5)


def packed(numbers):
    return sum(n << 2 * i for i, n in enumerate(numbers))


STEPS = sorted(((dx, dy) for dx in range(4) for dy in range(4)),
               key=lambda s: -min(s[0], 4 - s[0]) - min(s[1], 4 - s[1]))
STEPS_X = packed(s[0] for s in STEPS[:15])
STEPS_Y = packed(s[1] for s in STEPS[:15])


def dot(a, b, dims):
    return lax.dot_general(a, b, dims, preferred_element_type=F32)


def side_by_side(parts):
    return jnp.concatenate(list(parts), axis=1)


def scratch_shapes():
    dma = pltpu.SemaphoreType.DMA

    def vm(*shape, dtype=BF):
        return pltpu.VMEM(shape, dtype)

    def per(make, levels):
        return [make(h) if h in levels else None for h in LEVELS]

    t = types.SimpleNamespace()
    low, high, every, lowered = range(0, 1), range(1, 5), range(0, 5), range(1, 4)
    t.v = per(lambda h: vm(256, 4096), every)
    t.u = per(lambda h: vm(256, 2048), range(0, 4))
    t.vblk = per(lambda h: vm(33, 256, 128), high)
    t.v_load = per(lambda h: dma(()), every)
    t.u_load = per(lambda h: dma(()), range(0, 4))
    t.v_send = per(lambda h: dma(()), range(2, 5))
    t.u_send = per(lambda h: dma(()), range(2, 4))
    t.v_fwd = per(lambda h: dma((2,)), high)
    t.u_fwd = per(lambda h: dma((2,)), lowered)
    t.side = vm(256, 128)
    t.side_load = dma(())
    t.r = vm(32, 128, 128)
    t.r_send = dma((16,))
    t.r_recv = dma((16,))
    t.zb = per(lambda h: vm(128, 128), range(2, 5))
    t.zb_send = per(lambda h: dma(()), range(2, 5))
    t.zb_recv = per(lambda h: dma(()), range(2, 5))
    t.bn = per(lambda h: vm(128, 128), high)
    t.bn_send = per(lambda h: dma(()), high)
    t.bn_recv = per(lambda h: dma(()), high)
    t.bh = per(lambda h: vm(2, 64, 128), high)
    t.b = per(lambda h: vm(32, 64, 128), high)
    t.b_swap = per(lambda h: dma((2,)), high)
    t.b_send = per(lambda h: dma(()), high)
    t.b_recv = per(lambda h: dma(()), high)
    t.up_out = per(lambda h: vm(16, 128 if h == 0 else 64, 128), range(0, 4))
    t.up_in = per(lambda h: vm(15, 128 if h == 0 else 64, 128), range(0, 4))
    t.up_send = per(lambda h: dma(()), range(0, 4))
    t.up_recv = per(lambda h: dma(()), range(0, 4))
    t.halves = vm(2, 64, 128)
    t.vb = per(lambda h: vm(2, 17, 64, 128), high)
    t.swap = per(lambda h: dma((2,)), high)
    t.vb_send = per(lambda h: dma(()), high)
    t.vb_recv = per(lambda h: dma((2, 16)), high)
    t.y = per(lambda h: vm(128 if h == 0 else 64, 256, dtype=F32), every)
    t.w = per(lambda h: vm(64, 256), high)
    t.sel_out = per(lambda h: vm(16, 128 if h == 1 else 64, 128), high)
    t.sel_in = per(lambda h: vm(15, 128 if h == 1 else 64, 128), high)
    t.sel_send = per(lambda h: dma(()), high)
    t.sel_recv = per(lambda h: dma(()), high)
    t.g_half = vm(2, 64, 128)
    t.g_swap = dma((2,))
    t.g = per(lambda h: vm(16, 128, 128) if h == 0 else vm(17, 64, 128), range(0, 4))
    t.g_send = per(lambda h: dma(()), range(0, 4))
    t.g_recv = per(lambda h: dma((16,)), range(0, 4))
    t.x_out = per(lambda h: vm(2, 16, 64, 128), high)
    t.x_in = per(lambda h: vm(15, 2, 64, 128), high)
    t.x_send = per(lambda h: dma(()), high)
    t.x_recv = per(lambda h: dma(()), high)
    t.x_sum = per(lambda h: vm(2, 64, 128, dtype=F32), high)
    t.x_full = per(lambda h: vm(2, 64, 128, dtype=F32), high)
    t.x_rows = per(lambda h: vm(128, 128, dtype=F32), high)
    t.xx = per(lambda h: dma((2,)), high)
    t.x0_out = vm(16, 2, 128, 128)
    t.x0_in = vm(16, 2, 128, 128)
    t.x0_sum = vm(2, 128, 128, dtype=F32)
    t.x0_send = dma((16,))
    t.x0_recv = dma((16,))
    return t


def flat(t):
    out = []
    for entry in vars(t).values():
        out += [e for e in entry if e is not None] if isinstance(entry, list) else [entry]
    return out


def unflat(t, refs):
    refs = iter(refs)
    s = types.SimpleNamespace()
    for name, entry in vars(t).items():
        if isinstance(entry, list):
            vars(s)[name] = [None if e is None else next(refs) for e in entry]
        else:
            vars(s)[name] = next(refs)
    return s


def kernel(*refs):
    sides = refs[0:5]
    invs = refs[5:10]
    lows = refs[10:14]
    maps = refs[14:18]
    out = refs[18]
    s = unflat(scratch_shapes(), refs[19:])

    leaf = lax.axis_index("leaf")
    f = lax.axis_index("front")
    z = leaf // 2
    c = leaf % 2
    other = 1 - c

    def dev(z_, c_, f_):
        return (2 * z_ + c_, f_)

    def remote(src, dst, send, recv, device):
        return pltpu.make_async_remote_copy(
            src_ref=src, dst_ref=dst, send_sem=send, recv_sem=recv,
            device_id=device, device_id_type=MESH)

    def wait(ref, sem):
        pltpu.make_async_copy(ref, ref, sem).wait()

    def loop(lo, hi, body):
        lax.fori_loop(lo, hi, lambda i, carry: (body(i), carry)[1], 0)

    fx, fy = f // 4, f % 4

    def step_of(k):
        if isinstance(k, int):
            return STEPS[k]
        return (STEPS_X >> 2 * k) % 4, (STEPS_Y >> 2 * k) % 4

    def plane(k):
        dx, dy = step_of(k)
        return (fx + dx) % 4 * 4 + (fy + dy) % 4

    def source(k):
        dx, dy = step_of(k)
        return (fx + 4 - dx) % 4 * 4 + (fy + 4 - dy) % 4

    def group(h):
        n = 2 ** (h - 1)
        zrel = z % n
        return n, zrel, z - zrel

    def own(ref):
        return ref.at[0, 0]

    def rows(first, count):
        return pl.ds(pl.multiple_of(first, count), count)

    def columns(ref, block, count=1):
        return ref[:, pl.ds(pl.multiple_of(block * 128, 128 * count), 128 * count)]

    side_copy = pltpu.make_async_copy(own(sides[0]), s.side, s.side_load)
    side_copy.start()
    barrier = pltpu.get_barrier_semaphore()

    def greet_plane(d):
        q = (c * FRONT + f + d) % (2 * FRONT)
        pl.semaphore_signal(barrier, inc=1, device_id=dev(z, q // FRONT, q % FRONT),
                            device_id_type=MESH)

    def greet_line(d):
        pl.semaphore_signal(barrier, inc=1, device_id=dev((z + d) % 8, c, f),
                            device_id_type=MESH)

    loop(1, 2 * FRONT, greet_plane)
    loop(1, 8, greet_line)
    load_v0 = pltpu.make_async_copy(own(invs[0]), s.v[0], s.v_load[0])
    load_u0 = pltpu.make_async_copy(own(lows[0]), s.u[0], s.u_load[0])
    load_v0.start()
    load_u0.start()
    for h in range(1, 5):
        n, zrel, _ = group(h)
        m = 256 >> h
        at = rows(c * 128 + zrel * m, m)
        pltpu.make_async_copy(own(invs[h]), s.v[h].at[at], s.v_load[h]).start()
        if h < 4:
            pltpu.make_async_copy(own(lows[h]), s.u[h].at[at], s.u_load[h]).start()
        if h > 1:
            pltpu.make_async_copy(own(sides[h]), s.zb[h].at[rows(zrel * m, m)], s.zb_recv[h]).start()
    side_copy.wait()
    for k in range(2):
        s.r[2 * f + k] = s.side[k * 128:(k + 1) * 128, :].astype(F32).T.astype(BF)
    for h in range(1, 5):
        s.vb[h][0, 16] = jnp.zeros((64, 128), BF)
        s.vb[h][1, 16] = jnp.zeros((64, 128), BF)
        s.vblk[h][32] = jnp.zeros((256, 128), BF)
        if h < 4:
            s.g[h][16] = jnp.zeros((64, 128), BF)
    pl.semaphore_wait(barrier, 31 + 7)

    def send_b0(k):
        to = plane(k)

        @pl.when(to > f)
        def _():
            mine = s.r.at[pl.ds(2 * f, 2)]
            remote(mine, mine, s.r_send.at[to], s.r_recv.at[f], dev(z, c, to)).start()

    loop(0, 15, send_b0)

    def block_owner(h, zr):
        n = 2 ** (h - 1)
        m = 256 >> h
        p = (2 * zr + c) * (32 >> h) + f // n
        return p % 2, p // 2, (f % n) * m

    def send_block_rows(h, src, zr):
        m = 256 >> h
        co, fo, row = block_owner(h, zr)
        dst = s.bn[h].at[rows(row, m)]
        here = jnp.logical_and(co == c, fo == f)

        @pl.when(here)
        def _():
            pltpu.make_async_copy(src, dst, s.bn_recv[h]).start()

        @pl.when(jnp.logical_not(here))
        def _():
            remote(src, dst, s.bn_send[h], s.bn_recv[h], dev(z, co, fo)).start()

    def gather_factor(h, ref, mine, send, load):
        n, zrel, zbase = group(h)
        m = 256 >> h
        dst = ref.at[rows(c * 128 + zrel * m, m)]
        for d in range(1, n):
            remote(own(mine), dst, send, load, dev(zbase + (zrel + d) % n, c, f)).start()

    def gather_level(h):
        gather_factor(h, s.v[h], invs[h], s.v_send[h], s.v_load[h])
        if h < 4:
            gather_factor(h, s.u[h], lows[h], s.u_send[h], s.u_load[h])

    def forward_factor(ref, load, fwd):
        part = ref.at[rows(c * 128, 128)]
        wait(part, load)
        remote(part, part, fwd.at[0], fwd.at[1], dev(z, other, f)).start()

    def forward_level(h):
        forward_factor(s.v[h], s.v_load[h], s.v_fwd[h])
        if h < 4:
            forward_factor(s.u[h], s.u_load[h], s.u_fwd[h])

    def have_forward(ref, fwd):
        wait(ref.at[rows(other * 128, 128)], fwd.at[1])

    send_block_rows(1, own(sides[1]), 0)
    for h in range(2, 5):
        n, zrel, zbase = group(h)
        m = 256 >> h
        for d in range(1, n):
            remote(own(sides[h]), s.zb[h].at[rows(zrel * m, m)], s.zb_send[h], s.zb_recv[h],
                   dev(zbase + (zrel + d) % n, c, f)).start()
    gather_level(2)
    forward_level(1)

    load_v0.wait()

    def y0_term(k):
        return dot(side_by_side([s.r[2 * k], s.r[2 * k + 1]]), columns(s.v[0], 2 * k, 2), NT)

    def y0_step(d, acc):
        k = f - d
        wait(s.r.at[pl.ds(0, 2)], s.r_recv.at[k])
        return acc + y0_term(k)

    y0 = lax.fori_loop(1, f + 1, y0_step, y0_term(f))
    s.y[0][...] = y0
    y0 = y0.astype(BF)
    load_u0.wait()

    def by_fours(body):
        loop(0, 3, lambda q: body([4 * q, 4 * q + 1, 4 * q + 2, 4 * q + 3]))
        body([12, 13, 14, 15])

    def here(k):
        return isinstance(k, int) and k == 15

    def up(h, y):
        def four(ks):
            part = dot(y, side_by_side(columns(s.u[h], plane(k)) for k in ks), NN).astype(BF)
            for n, k in enumerate(ks):
                i = plane(k)
                s.up_out[h][i] = part[:, n * 128:(n + 1) * 128]
                if not here(k):
                    remote(s.up_out[h].at[i], s.up_in[h].at[k], s.up_send[h], s.up_recv[h],
                           dev(z, c, i)).start()

        by_fours(four)

    up(0, y0)

    def turn_b(h):
        wait(s.bn[h], s.bn_recv[h])
        turned = s.bn[h][...].astype(F32).T.astype(BF)
        s.bh[h][0] = turned[:64]
        s.bh[h][1] = turned[64:]
        block = 2 * f + c
        s.b[h][block] = s.bh[h][c]
        remote(s.bh[h].at[other], s.b[h].at[block], s.b_swap[h].at[0], s.b_swap[h].at[1],
               dev(z, other, f)).start()

    def spread_b(h):
        wait(s.b[h].at[0], s.b_swap[h].at[1])
        both = s.b[h].at[pl.ds(2 * f, 2)]
        loop(0, 15, lambda k: remote(both, both, s.b_send[h], s.b_recv[h],
                                     dev(z, c, plane(k))).start())

    def split_columns(h):
        have_forward(s.v[h], s.v_fwd[h])

        def one(k):
            s.vblk[h][k] = columns(s.v[h], k)

        loop(0, 32, one)

    turn_b(1)
    for h in range(2, 5):
        m = 256 >> h
        wait(s.zb[h], s.zb_recv[h])
        for zr in range(2 ** (h - 1)):
            send_block_rows(h, s.zb[h].at[pl.ds(zr * m, m)], zr)
    gather_level(3)
    split_columns(1)
    spread_b(1)

    def send_child(h, child, kind):
        at = s.vb[h].at[child, f]
        loop(0, 15, lambda k: remote(at, at, s.vb_send[h], s.vb_recv[h].at[kind, f],
                                     dev(z, c, plane(k))).start())

    def side_term(h):
        wait(s.b[h].at[pl.ds(0, 30)], s.b_recv[h])

        def step(j, acc):
            part = side_by_side(s.b[h][8 * j + k] for k in range(8))
            return acc + dot(part, columns(s.v[h], 8 * j, 8), NT)

        return lax.fori_loop(0, 4, step, jnp.zeros((64, 256), F32))

    def child_term(h, child, kind, acc):
        table = maps[h - 1]
        row = 2 * (z // 2 ** (h - 1)) + child

        def pair(ks):
            at = [jnp.minimum(table[row, k], 32) for k in ks]
            return dot(side_by_side(s.vb[h][child, k] for k in ks),
                       side_by_side(s.vblk[h][a] for a in at), NT)

        def arrived(k):
            wait(s.vb[h].at[0, 0], s.vb_recv[h].at[kind, source(k)])

        def step(q, acc):
            arrived(14 - 2 * q)
            arrived(13 - 2 * q)
            return acc - pair([source(14 - 2 * q), source(13 - 2 * q)])

        acc = lax.fori_loop(0, 7, step, acc)
        arrived(0)
        return acc - pair([f, source(0)])

    def bottom_block(h, child):
        table = maps[h - 1]
        row = 2 * (z // 2 ** (h - 1)) + child
        less = jnp.int32(0)
        hit = jnp.int32(0)
        for i in range(16):
            less = less + (table[row, i] < 32 + f).astype(jnp.int32)
            hit = hit + (table[row, i] == 32 + f).astype(jnp.int32)
        return jnp.where(hit > 0, less, 16)

    def summed(ref, first):
        total = first
        for k in range(15):
            total = total + ref[k].astype(F32)
        return total

    def give_blocks(h, mine, half, sibling):
        remote(half, s.vb[h].at[mine, f], s.swap[h].at[0], s.swap[h].at[1], sibling).start()
        send_child(h, mine, 0)
        wait(s.vb[h].at[mine, f], s.swap[h].at[1])
        send_child(h, 1 - mine, 1)

    wait(s.up_in[0], s.up_recv[0])
    total = summed(s.up_in[0], s.up_out[0][f].astype(F32)).astype(BF)
    s.halves[0] = total[:64]
    s.halves[1] = total[64:]
    s.vb[1][c, f] = s.halves[c]
    give_blocks(1, c, s.halves.at[other], dev(z, other, f))
    for h in range(2, 5):
        turn_b(h)

    for h in range(1, 5):
        mine = c if h == 1 else z // 2 ** (h - 2) % 2
        acc = side_term(h)
        acc = child_term(h, mine, 0, acc)
        acc = child_term(h, 1 - mine, 1, acc)
        s.y[h][...] = acc
        y = acc.astype(BF)
        if h == 4:
            s.w[4][...] = y
            break
        have_forward(s.u[h], s.u_fwd[h])
        up(h, y)
        spread_b(h + 1)
        forward_level(h + 1)
        bottom = [bottom_block(h, child) for child in range(2)]
        split_columns(h + 1)
        kept = s.vb[h][0, bottom[0]].astype(F32) + s.vb[h][1, bottom[1]].astype(F32)
        kept = kept + s.up_out[h][f].astype(F32)
        wait(s.up_in[h], s.up_recv[h])
        step = 2 ** (h - 1)
        mine = z // step % 2
        s.vb[h + 1][mine, f] = summed(s.up_in[h], kept).astype(BF)
        give_blocks(h + 1, mine, s.vb[h + 1].at[mine, f], dev(z + step - 2 * step * mine, c, f))
        if h == 1:
            gather_level(4)

    def take_x(h):
        wait(s.x_in[h], s.x_recv[h])
        n = 2 ** (h - 1)
        s.x_sum[h][...] = summed(s.x_in[h], s.x_out[h][:, f // n].astype(F32))
        s.x_full[h][c] = s.x_sum[h][c]
        remote(s.x_sum[h].at[other], s.x_full[h].at[c], s.xx[h].at[0], s.xx[h].at[1],
               dev(z, other, f)).start()

    def give_x(h):
        wait(s.x_full[h].at[0], s.xx[h].at[1])
        n = 2 ** (h - 1)
        m = 256 >> h
        s.x_rows[h][...] = s.x_full[h][...].reshape(128, 128).T
        out[m:2 * m, :] = s.x_rows[h][rows((f % n) * m, m), :]

    def reaction(h):
        def pair(ks):
            return dot(side_by_side(s.g[h][k] for k in ks),
                       side_by_side(columns(s.u[h], k) for k in ks), NT)

        def arrived(k):
            wait(s.g[h].at[0], s.g_recv[h].at[source(k)])

        def step(q, acc):
            arrived(14 - 2 * q)
            arrived(13 - 2 * q)
            return acc + pair([source(14 - 2 * q), source(13 - 2 * q)])

        acc = lax.fori_loop(0, 7, step, jnp.zeros(s.y[h].shape, F32))
        arrived(0)
        return acc + pair([f, source(0)])

    def send_g(h):
        at = s.g[h].at[f]
        loop(0, 15, lambda k: remote(at, at, s.g_send[h], s.g_recv[h].at[f],
                                     dev(z, c, plane(k))).start())

    for h in range(4, 0, -1):
        if h < 4:
            s.w[h][...] = (s.y[h][...] - reaction(h)).astype(BF)
        table = maps[h - 1]
        first = 2 * z if h == 1 else z // 2 ** (h - 2)

        def select(ks, child, h=h, table=table, first=first):
            at = [table[first + child, plane(k)] for k in ks]
            part = dot(s.w[h][...], side_by_side(s.vblk[h][jnp.minimum(a, 32)] for a in at), NN)
            blocks = [part[:, n * 128:(n + 1) * 128] for n in range(4)]
            if here(ks[3]) and h < 4:
                kept = jnp.where(at[3] >= 32, at[3] - 32, 16)
                blocks[3] = blocks[3] + s.g[h][kept].astype(F32)
            return blocks

        def down(ks, h=h, select=select):
            for child in range(2 if h == 1 else 1):
                for k, block in zip(ks, select(ks, child)):
                    s.sel_out[h][plane(k), child * 64:(child + 1) * 64] = block.astype(BF)
            for k in ks:
                i = plane(k)
                if not here(k):
                    remote(s.sel_out[h].at[i], s.sel_in[h].at[k], s.sel_send[h], s.sel_recv[h],
                           dev(z, c, i)).start()

        by_fours(down)

        n, zrel, _ = group(h)
        half = 32 >> h
        for part in range(2):
            def x_step(q, h=h, half=half, zrel=zrel, part=part):
                both = dot(s.w[h][...], columns(s.v[h], zrel * 2 * half + part * half + 2 * q, 2),
                           NN).astype(BF)
                s.x_out[h][part, 2 * q] = both[:, :128]
                s.x_out[h][part, 2 * q + 1] = both[:, 128:]

            loop(0, half // 2, x_step)

        def send_x(k, h=h, n=n):
            remote(s.x_out[h].at[:, plane(k) // n], s.x_in[h].at[k], s.x_send[h],
                   s.x_recv[h], dev(z, c, plane(k))).start()

        loop(0, 15, send_x)
        if h < 4:
            take_x(h + 1)

        wait(s.sel_in[h], s.sel_recv[h])
        total = summed(s.sel_in[h], s.sel_out[h][f].astype(F32)).astype(BF)
        if h > 1:
            s.g[h - 1][f] = total
        else:
            s.g_half[0] = total[:64]
            s.g_half[1] = total[64:]
            half = s.g[0].at[f, rows(c * 64, 64)]
            s.g[0][f, rows(c * 64, 64)] = s.g_half[c]
            remote(s.g_half.at[other], half, s.g_swap.at[0], s.g_swap.at[1],
                   dev(z, other, f)).start()
            wait(half, s.g_swap.at[1])
        send_g(h - 1)
        if h < 4:
            give_x(h + 1)

    w0 = (s.y[0][...] - reaction(0)).astype(BF)

    def x0_block(k):
        return dot(w0, columns(s.v[0], 2 * k, 2), NN)

    def x0_give(k):
        both = x0_block(k).astype(BF)
        s.x0_out[k, 0] = both[:, :128]
        s.x0_out[k, 1] = both[:, 128:]
        remote(s.x0_out.at[k], s.x0_in.at[f], s.x0_send.at[k], s.x0_recv.at[f],
               dev(z, c, k)).start()

    def x0_maybe(k):
        to = plane(k)

        @pl.when(to < f)
        def _():
            x0_give(to)

    loop(0, 15, x0_maybe)
    mine = x0_block(f)
    s.x0_sum[0] = mine[:, :128]
    s.x0_sum[1] = mine[:, 128:]
    take_x(1)

    def x0_take(k):
        wait(s.x0_in.at[k], s.x0_recv.at[k])
        s.x0_sum[...] = s.x0_sum[...] + s.x0_in[k].astype(F32)

    loop(f + 1, FRONT, x0_take)
    for k in range(2):
        out[256 + k * 128:256 + (k + 1) * 128, :] = s.x0_sum[k].T
    give_x(1)

    loop(0, f, lambda k: wait(s.x0_out.at[k], s.x0_send.at[k]))
    loop(f + 1, FRONT, lambda k: wait(s.r.at[pl.ds(0, 2)], s.r_send.at[k]))
    wait(s.up_in[0], s.up_send[0])
    wait(s.g_half.at[0], s.g_swap.at[0])
    wait(s.g[0].at[pl.ds(0, 15)], s.g_send[0])
    for h in range(1, 5):
        n = 2 ** (h - 1)
        m = 256 >> h
        wait(s.v[h].at[pl.ds(0, 128)], s.v_fwd[h].at[0])
        if h < 4:
            wait(s.u[h].at[pl.ds(0, 128)], s.u_fwd[h].at[0])
        if n > 1:
            wait(s.v[h].at[pl.ds(0, (n - 1) * m)], s.v_send[h])
            if h < 4:
                wait(s.u[h].at[pl.ds(0, (n - 1) * m)], s.u_send[h])
            wait(s.zb[h].at[pl.ds(0, (n - 1) * m)], s.zb_send[h])
        away = jnp.int32(0)
        for zr in range(n):
            co, fo, _ = block_owner(h, zr)
            away = away + jnp.where(jnp.logical_and(co == c, fo == f), 0, 1)
        for count in range(max(n - 1, 1), n + 1):
            @pl.when(away == count)
            def _(count=count, h=h, m=m):
                wait(s.bn[h].at[pl.ds(0, count * m)], s.bn_send[h])
        wait(s.b[h].at[pl.ds(0, 30)], s.b_send[h])
        wait(s.b[h].at[0], s.b_swap[h].at[0])
        wait(s.vb[h].at[0, 0], s.swap[h].at[0])
        wait(s.sel_in[h], s.sel_send[h])
        wait(s.vb[h].at[:, pl.ds(0, 15)], s.vb_send[h])
        wait(s.x_in[h], s.x_send[h])
        wait(s.x_sum[h].at[0], s.xx[h].at[0])
        if h < 4:
            wait(s.up_in[h], s.up_send[h])
            wait(s.g[h].at[pl.ds(0, 15)], s.g_send[h])


def hand_out(packed_rows, *refs):
    outs, sems = refs[:5], refs[5]
    copies = [pltpu.make_async_copy(packed_rows.at[pl.ds(256 >> h, 256 >> h)], outs[h].at[0, 0],
                                    sems.at[h]) for h in LEVELS]
    for copy in copies:
        copy.start()
    for copy in copies:
        copy.wait()


def on_device(*args):
    in_hbm = pl.BlockSpec(memory_space=pltpu.HBM)
    smem = pl.BlockSpec(memory_space=pltpu.SMEM)
    vmem = pl.BlockSpec(memory_space=pltpu.VMEM)
    packed_rows = pl.pallas_call(
        kernel,
        out_shape=jax.ShapeDtypeStruct((512, 128), F32),
        in_specs=[in_hbm] * 14 + [smem] * 4,
        out_specs=vmem,
        scratch_shapes=flat(scratch_shapes()),
        compiler_params=pltpu.CompilerParams(
            collective_id=0, has_side_effects=True, vmem_limit_bytes=56 * 2 ** 20),
        name="solve",
    )(*args)
    return tuple(pl.pallas_call(
        hand_out,
        out_shape=[jax.ShapeDtypeStruct(a.shape, F32) for a in args[:5]],
        in_specs=[vmem],
        out_specs=[in_hbm] * 5,
        scratch_shapes=[pltpu.SemaphoreType.DMA((5,))],
        name="hand_out",
    )(packed_rows))


def solution(mesh):
    shard = P("leaf", "front", None, None)
    return jax.shard_map(
        on_device,
        mesh=mesh,
        in_specs=(shard,) * 14 + (P(),) * 4,
        out_specs=(shard,) * 5,
        check_vma=False,
    )
```

time: 1570 us -> 198 us (0.13)
  waiting for transfers between devices: 1090 us -> 0 us
  blocking collectives: 206 us -> 0 us
  Pallas kernels: 0 us -> 197 us
  starting transfers between devices: 150 us -> 0 us
  local copies, waits for them, and re-layouts: 48.6 us -> 0 us
  other arithmetic: 32.6 us -> 0 us
  matrix products: 20 us -> 0 us
    unnamed x19 -> x0, waiting for transfers between devices: 687 us -> none
    ppermute x46 -> x0, waiting for transfers between devices: 350 us -> none  [swapped(): return lax.ppermute(value, axis, pairs)]
    all_gather x12 -> x0, blocking collectives: 206 us -> none  [group_gather(): gathered = lax.all_gather(pieces, 'front', axis=1, tiled=True)]
    pallas_call x0 -> x2, Pallas kernels: none -> 197 us  [the longest x1 195 us: on_device(): pl.pallas_call(kernel, out_shape=jax.ShapeDtypeStruct((512, 128), F32), i...]
    ppermute x46 -> x0, starting transfers between devices: 149 us -> none  [swapped(): return lax.ppermute(value, axis, pairs)]
    all_gather x1 -> x0, waiting for transfers between devices: 50.3 us -> none  [group_gather(): gathered = lax.all_gather(pieces, 'front', axis=1, tiled=True)]
    dot_general x17 -> x0, matrix products: 20 us -> none  [the longest x5 11.4 us: solve(): jnp.einsum('fmp,fmr->fpr', factor, adjusted, preferred_element_type=jnp.f...]
  transfers between devices with their start and end apart: 56 -> 0, of which waited for: 54 -> 0; matrix products, arithmetic and copies ran while one was open for 2% -> 0% of each run, Pallas kernels for 0% -> 0%
where the time goes in v1:
time: 198 us; the launch traced here: 197 us
  Pallas kernels  197 us (99%)
    pallas_call x1, Pallas kernels, on_device(): pl.pallas_call(kernel, out_shape=jax.ShapeDtypeStruct((512, 128), F32), i...  195 us

profile of v1, /device:TPU:1, one launch (start us, length us, event | category | flops | bytes accessed | tf_op | source)
XLA Modules:
  0.0 197.4 jit_solution(11290656292076944929)
XLA Ops:
  0.6 195.1 %solve.1.packed_rows = f32[512,128]{1,0:T(8,128)} custom-call(bf16[1,1,256,128]{3,2,1,0:T(8,128)(2,1)} %refs_0_.1, bf16[1,1,128,128]{3,2,1,0:T(8,128)(2,1)} %refs_1_.1, bf16[1,1,64,128]{3,2,1,0:T(8,128)(2,1)} %refs_2_.1, bf16[1,1,32,128]{3,2,1,0:T(8,128)(2,1)} %refs_3_.1, bf16[1,1,16,128]{3,2,1,0:T(8,128)(2,1)} %refs_4_.1, ...), custom_call_target="tpu_custom_call" | custom-call | tf_op jit(solution)/shard_map/solve/pallas_call | solution.py:633
  195.7 1.7 hand_out.1

commit v2 on v1

--- a/solution.py
+++ b/solution.py
@@ -14,6 +14,7 @@
 NN = (((1,), (0,)), ((), ()))
 FRONT = 16
 LEVELS = range(5)
+SHARE = (128, 64, 32, 16, 16)
 
 
 def packed(numbers):
@@ -51,6 +52,7 @@
     t.v_load = per(lambda h: dma(()), every)
     t.u_load = per(lambda h: dma(()), range(0, 4))
     t.v_send = per(lambda h: dma(()), range(2, 5))
+    t.v_ring = dma((8,))
     t.u_send = per(lambda h: dma(()), range(2, 4))
     t.v_fwd = per(lambda h: dma((2,)), high)
     t.u_fwd = per(lambda h: dma((2,)), lowered)
@@ -65,24 +67,29 @@
     t.bn = per(lambda h: vm(128, 128), high)
     t.bn_send = per(lambda h: dma(()), high)
     t.bn_recv = per(lambda h: dma(()), high)
-    t.bh = per(lambda h: vm(2, 64, 128), high)
-    t.b = per(lambda h: vm(32, 64, 128), high)
+    t.bh = per(lambda h: vm(128 // SHARE[h], SHARE[h], 128), high)
+    t.b = per(lambda h: vm(32, SHARE[h], 128), high)
     t.b_swap = per(lambda h: dma((2,)), high)
     t.b_send = per(lambda h: dma(()), high)
     t.b_recv = per(lambda h: dma(()), high)
-    t.up_out = per(lambda h: vm(16, 128 if h == 0 else 64, 128), range(0, 4))
-    t.up_in = per(lambda h: vm(15, 128 if h == 0 else 64, 128), range(0, 4))
+    t.up_out = per(lambda h: vm(16, SHARE[h], 128), range(0, 4))
+    t.up_in = per(lambda h: vm(15, SHARE[h], 128), range(0, 4))
     t.up_send = per(lambda h: dma(()), range(0, 4))
     t.up_recv = per(lambda h: dma(()), range(0, 4))
-    t.halves = vm(2, 64, 128)
-    t.vb = per(lambda h: vm(2, 17, 64, 128), high)
+    t.halves = per(lambda h: vm(2, SHARE[h], 128), lowered)
+    t.vb = per(lambda h: vm(2, 17, SHARE[h], 128), high)
     t.swap = per(lambda h: dma((2,)), high)
     t.vb_send = per(lambda h: dma(()), high)
     t.vb_recv = per(lambda h: dma((2, 16)), high)
-    t.y = per(lambda h: vm(128 if h == 0 else 64, 256, dtype=F32), every)
+    t.y = per(lambda h: vm(SHARE[h], 256, dtype=F32), range(0, 2))
+    t.yz = per(lambda h: vm(64 // SHARE[h], SHARE[h], 256, dtype=F32), range(2, 5))
+    t.yz_send = per(lambda h: dma(()), range(2, 5))
+    t.yz_recv = per(lambda h: dma(()), range(2, 5))
     t.w = per(lambda h: vm(64, 256), high)
-    t.sel_out = per(lambda h: vm(16, 128 if h == 1 else 64, 128), high)
-    t.sel_in = per(lambda h: vm(15, 128 if h == 1 else 64, 128), high)
+    t.w4 = vm(16, 256)
+    t.sel_out = per(lambda h: vm(16, (0, 128, 64, 64, 16)[h], 128), high)
+    t.sel_in = per(lambda h: vm(15, (0, 128, 64, 64, 16)[h], 128), high)
+    t.gz = dma((2,))
     t.sel_send = per(lambda h: dma(()), high)
     t.sel_recv = per(lambda h: dma(()), high)
     t.g_half = vm(2, 64, 128)
@@ -172,6 +179,9 @@
         zrel = z % n
         return n, zrel, z - zrel
 
+    def share(h):
+        return (0, 0, z % 2, z % 2 * 2 + z // 2 % 2, z % 2 * 2 + z // 2 % 2)[h]
+
     def own(ref):
         return ref.at[0, 0]
 
@@ -213,8 +223,8 @@
     for k in range(2):
         s.r[2 * f + k] = s.side[k * 128:(k + 1) * 128, :].astype(F32).T.astype(BF)
     for h in range(1, 5):
-        s.vb[h][0, 16] = jnp.zeros((64, 128), BF)
-        s.vb[h][1, 16] = jnp.zeros((64, 128), BF)
+        s.vb[h][0, 16] = jnp.zeros((SHARE[h], 128), BF)
+        s.vb[h][1, 16] = jnp.zeros((SHARE[h], 128), BF)
         s.vblk[h][32] = jnp.zeros((256, 128), BF)
         if h < 4:
             s.g[h][16] = jnp.zeros((64, 128), BF)
@@ -259,16 +269,43 @@
 
     def gather_level(h):
         gather_factor(h, s.v[h], invs[h], s.v_send[h], s.v_load[h])
-        if h < 4:
-            gather_factor(h, s.u[h], lows[h], s.u_send[h], s.u_load[h])
+        gather_factor(h, s.u[h], lows[h], s.u_send[h], s.u_load[h])
 
     def forward_factor(ref, load, fwd):
         part = ref.at[rows(c * 128, 128)]
-        wait(part, load)
+        if load is not None:
+            wait(part, load)
         remote(part, part, fwd.at[0], fwd.at[1], dev(z, other, f)).start()
 
+    def ring(step):
+        def rows_of(d):
+            return s.v[4].at[rows(c * 128 + (z + 8 + d) % 8 * 16, 16)]
+
+        def pass_on(d, to):
+            remote(rows_of(d), rows_of(d), s.v_send[4], s.v_ring.at[(z + 8 + d) % 8],
+                   dev((z + 8 + to) % 8, c, f)).start()
+
+        def arrived(d):
+            wait(rows_of(d), s.v_ring.at[(z + 8 + d) % 8])
+
+        if step == 1:
+            wait(rows_of(0), s.v_load[4])
+            pass_on(0, 1)
+            pass_on(0, -1)
+        elif step < 4:
+            arrived(1 - step)
+            pass_on(1 - step, 1)
+            arrived(step - 1)
+            pass_on(step - 1, -1)
+        elif step == 4:
+            arrived(-3)
+            pass_on(-3, 1)
+        else:
+            arrived(3)
+            arrived(-4)
+
     def forward_level(h):
-        forward_factor(s.v[h], s.v_load[h], s.v_fwd[h])
+        forward_factor(s.v[h], s.v_load[h] if h < 4 else None, s.v_fwd[h])
         if h < 4:
             forward_factor(s.u[h], s.u_load[h], s.u_fwd[h])
 
@@ -283,6 +320,7 @@
             remote(own(sides[h]), s.zb[h].at[rows(zrel * m, m)], s.zb_send[h], s.zb_recv[h],
                    dev(zbase + (zrel + d) % n, c, f)).start()
     gather_level(2)
+    gather_level(3)
     forward_level(1)
 
     load_v0.wait()
@@ -324,12 +362,12 @@
     def turn_b(h):
         wait(s.bn[h], s.bn_recv[h])
         turned = s.bn[h][...].astype(F32).T.astype(BF)
-        s.bh[h][0] = turned[:64]
-        s.bh[h][1] = turned[64:]
+        s.bh[h][...] = turned.reshape(s.bh[h].shape)
         block = 2 * f + c
-        s.b[h][block] = s.bh[h][c]
-        remote(s.bh[h].at[other], s.b[h].at[block], s.b_swap[h].at[0], s.b_swap[h].at[1],
-               dev(z, other, f)).start()
+        shares = 64 // SHARE[h]
+        s.b[h][block] = s.bh[h][c * shares + share(h)]
+        remote(s.bh[h].at[other * shares + share(h)], s.b[h].at[block], s.b_swap[h].at[0],
+               s.b_swap[h].at[1], dev(z, other, f)).start()
 
     def spread_b(h):
         wait(s.b[h].at[0], s.b_swap[h].at[1])
@@ -351,7 +389,6 @@
         wait(s.zb[h], s.zb_recv[h])
         for zr in range(2 ** (h - 1)):
             send_block_rows(h, s.zb[h].at[pl.ds(zr * m, m)], zr)
-    gather_level(3)
     split_columns(1)
     spread_b(1)
 
@@ -367,7 +404,7 @@
             part = side_by_side(s.b[h][8 * j + k] for k in range(8))
             return acc + dot(part, columns(s.v[h], 8 * j, 8), NT)
 
-        return lax.fori_loop(0, 4, step, jnp.zeros((64, 256), F32))
+        return lax.fori_loop(0, 4, step, jnp.zeros((SHARE[h], 256), F32))
 
     def child_term(h, child, kind, acc):
         table = maps[h - 1]
@@ -414,10 +451,9 @@
 
     wait(s.up_in[0], s.up_recv[0])
     total = summed(s.up_in[0], s.up_out[0][f].astype(F32)).astype(BF)
-    s.halves[0] = total[:64]
-    s.halves[1] = total[64:]
-    s.vb[1][c, f] = s.halves[c]
-    give_blocks(1, c, s.halves.at[other], dev(z, other, f))
+    s.halves[1][...] = total.reshape(2, 64, 128)
+    s.vb[1][c, f] = s.halves[1][c]
+    give_blocks(1, c, s.halves[1].at[other], dev(z, other, f))
     for h in range(2, 5):
         turn_b(h)
 
@@ -426,26 +462,49 @@
         acc = side_term(h)
         acc = child_term(h, mine, 0, acc)
         acc = child_term(h, 1 - mine, 1, acc)
-        s.y[h][...] = acc
         y = acc.astype(BF)
+        if h == 1:
+            s.y[1][...] = acc
+        else:
+            n = 64 // SHARE[h]
+            mine = s.yz[h].at[share(h)]
+            s.yz[h][share(h)] = acc
+            for d in range(1, n):
+                remote(mine, mine, s.yz_send[h], s.yz_recv[h],
+                       dev(z - z % n + (z + d) % n, c, f)).start()
         if h == 4:
-            s.w[4][...] = y
+            s.w4[...] = y
             break
         have_forward(s.u[h], s.u_fwd[h])
         up(h, y)
         spread_b(h + 1)
-        forward_level(h + 1)
+        if h < 3:
+            forward_level(h + 1)
+        if h > 1:
+            ring(2 * h - 2)
         bottom = [bottom_block(h, child) for child in range(2)]
-        split_columns(h + 1)
+        if h < 3:
+            split_columns(h + 1)
         kept = s.vb[h][0, bottom[0]].astype(F32) + s.vb[h][1, bottom[1]].astype(F32)
         kept = kept + s.up_out[h][f].astype(F32)
         wait(s.up_in[h], s.up_recv[h])
         step = 2 ** (h - 1)
         mine = z // step % 2
-        s.vb[h + 1][mine, f] = summed(s.up_in[h], kept).astype(BF)
-        give_blocks(h + 1, mine, s.vb[h + 1].at[mine, f], dev(z + step - 2 * step * mine, c, f))
-        if h == 1:
-            gather_level(4)
+        total = summed(s.up_in[h], kept).astype(BF)
+        if h < 3:
+            s.halves[h + 1][...] = total.reshape(s.halves[h + 1].shape)
+            s.vb[h + 1][mine, f] = s.halves[h + 1][mine]
+            half = s.halves[h + 1].at[1 - mine]
+        else:
+            s.vb[4][mine, f] = total
+            half = s.vb[4].at[mine, f]
+        give_blocks(h + 1, mine, half, dev(z + step - 2 * step * mine, c, f))
+        if h < 3:
+            ring(2 * h - 1)
+        else:
+            ring(5)
+            forward_level(4)
+            split_columns(4)
 
     def take_x(h):
         wait(s.x_in[h], s.x_recv[h])
@@ -475,9 +534,24 @@
             arrived(13 - 2 * q)
             return acc + pair([source(14 - 2 * q), source(13 - 2 * q)])
 
-        acc = lax.fori_loop(0, 7, step, jnp.zeros(s.y[h].shape, F32))
+        acc = lax.fori_loop(0, 7, step, jnp.zeros((128 if h == 0 else 64, 256), F32))
         arrived(0)
         return acc + pair([f, source(0)])
+
+    def send_rows(h):
+        n, zrel, _ = group(h)
+        half = 32 >> h
+        for part in range(2):
+            def x_step(q, part=part):
+                both = dot(s.w[h][...], columns(s.v[h], zrel * 2 * half + part * half + 2 * q, 2),
+                           NN).astype(BF)
+                s.x_out[h][part, 2 * q] = both[:, :128]
+                s.x_out[h][part, 2 * q + 1] = both[:, 128:]
+
+            loop(0, half // 2, x_step)
+
+        loop(0, 15, lambda k: remote(s.x_out[h].at[:, plane(k) // n], s.x_in[h].at[k], s.x_send[h],
+                                     s.x_recv[h], dev(z, c, plane(k))).start())
 
     def send_g(h):
         at = s.g[h].at[f]
@@ -485,14 +559,19 @@
                                      dev(z, c, plane(k))).start())
 
     for h in range(4, 0, -1):
-        if h < 4:
-            s.w[h][...] = (s.y[h][...] - reaction(h)).astype(BF)
+        if h == 1:
+            s.w[1][...] = (s.y[1][...] - reaction(1)).astype(BF)
+        elif h < 4:
+            react = reaction(h)
+            wait(s.yz[h].at[pl.ds(1, 64 // SHARE[h] - 1)], s.yz_recv[h])
+            s.w[h][...] = (s.yz[h][...].reshape(64, 256) - react).astype(BF)
+        w_sel = s.w4 if h == 4 else s.w[h]
         table = maps[h - 1]
         first = 2 * z if h == 1 else z // 2 ** (h - 2)
 
-        def select(ks, child, h=h, table=table, first=first):
+        def select(ks, child, h=h, table=table, first=first, w_sel=w_sel):
             at = [table[first + child, plane(k)] for k in ks]
-            part = dot(s.w[h][...], side_by_side(s.vblk[h][jnp.minimum(a, 32)] for a in at), NN)
+            part = dot(w_sel[...], side_by_side(s.vblk[h][jnp.minimum(a, 32)] for a in at), NN)
             blocks = [part[:, n * 128:(n + 1) * 128] for n in range(4)]
             if here(ks[3]) and h < 4:
                 kept = jnp.where(at[3] >= 32, at[3] - 32, 16)
@@ -502,7 +581,8 @@
         def down(ks, h=h, select=select):
             for child in range(2 if h == 1 else 1):
                 for k, block in zip(ks, select(ks, child)):
-                    s.sel_out[h][plane(k), child * 64:(child + 1) * 64] = block.astype(BF)
+                    n = block.shape[0]
+                    s.sel_out[h][plane(k), child * n:(child + 1) * n] = block.astype(BF)
             for k in ks:
                 i = plane(k)
                 if not here(k):
@@ -511,28 +591,20 @@
 
         by_fours(down)
 
-        n, zrel, _ = group(h)
-        half = 32 >> h
-        for part in range(2):
-            def x_step(q, h=h, half=half, zrel=zrel, part=part):
-                both = dot(s.w[h][...], columns(s.v[h], zrel * 2 * half + part * half + 2 * q, 2),
-                           NN).astype(BF)
-                s.x_out[h][part, 2 * q] = both[:, :128]
-                s.x_out[h][part, 2 * q + 1] = both[:, 128:]
-
-            loop(0, half // 2, x_step)
-
-        def send_x(k, h=h, n=n):
-            remote(s.x_out[h].at[:, plane(k) // n], s.x_in[h].at[k], s.x_send[h],
-                   s.x_recv[h], dev(z, c, plane(k))).start()
-
-        loop(0, 15, send_x)
+        if h < 4:
+            send_rows(h)
         if h < 4:
             take_x(h + 1)
 
         wait(s.sel_in[h], s.sel_recv[h])
         total = summed(s.sel_in[h], s.sel_out[h][f].astype(F32)).astype(BF)
-        if h > 1:
+        if h == 4:
+            mine = s.g[3].at[f, rows(share(4) * 16, 16)]
+            s.g[3][f, rows(share(4) * 16, 16)] = total
+            for d in range(1, 4):
+                remote(mine, mine, s.gz.at[0], s.gz.at[1], dev(z - z % 4 + (z + d) % 4, c, f)).start()
+            wait(s.g[3].at[f, pl.ds(0, 48)], s.gz.at[1])
+        elif h > 1:
             s.g[h - 1][f] = total
         else:
             s.g_half[0] = total[:64]
@@ -545,6 +617,10 @@
         send_g(h - 1)
         if h < 4:
             give_x(h + 1)
+        else:
+            wait(s.yz[4].at[pl.ds(1, 3)], s.yz_recv[4])
+            s.w[4][...] = s.yz[4][...].reshape(64, 256).astype(BF)
+            send_rows(4)
 
     w0 = (s.y[0][...] - reaction(0)).astype(BF)
 
@@ -584,6 +660,7 @@
     loop(f + 1, FRONT, lambda k: wait(s.r.at[pl.ds(0, 2)], s.r_send.at[k]))
     wait(s.up_in[0], s.up_send[0])
     wait(s.g_half.at[0], s.g_swap.at[0])
+    wait(s.g[3].at[f, pl.ds(0, 48)], s.gz.at[0])
     wait(s.g[0].at[pl.ds(0, 15)], s.g_send[0])
     for h in range(1, 5):
         n = 2 ** (h - 1)
@@ -608,6 +685,8 @@
         wait(s.b[h].at[0], s.b_swap[h].at[0])
         wait(s.vb[h].at[0, 0], s.swap[h].at[0])
         wait(s.sel_in[h], s.sel_send[h])
+        if h > 1:
+            wait(s.yz[h].at[pl.ds(1, 64 // SHARE[h] - 1)], s.yz_send[h])
         wait(s.vb[h].at[:, pl.ds(0, 15)], s.vb_send[h])
         wait(s.x_in[h], s.x_send[h])
         wait(s.x_sum[h].at[0], s.xx[h].at[0])

time: 198 us -> 184 us (0.929)
  Pallas kernels: 197 us -> 184 us
    pallas_call x1, Pallas kernels: 195 us -> 182 us  [on_device(): pl.pallas_call(kernel, out_shape=jax.ShapeDtypeStruct((512, 128), F32), i...]
where the time goes in v2:
time: 184 us
  Pallas kernels  184 us (100%)
    pallas_call x1, Pallas kernels, on_device(): pl.pallas_call(kernel, out_shape=jax.ShapeDtypeStruct((512, 128), F32), i...  182 us

profile of v2, /device:TPU:1, one launch (start us, length us, event | category | flops | bytes accessed | tf_op | source)
XLA Modules:
  0.0 184.3 jit_solution(769649108194302748)
XLA Ops:
  0.6 182.0 %solve.1.packed_rows = f32[512,128]{1,0:T(8,128)} custom-call(bf16[1,1,256,128]{3,2,1,0:T(8,128)(2,1)} %refs_0_.1, bf16[1,1,128,128]{3,2,1,0:T(8,128)(2,1)} %refs_1_.1, bf16[1,1,64,128]{3,2,1,0:T(8,128)(2,1)} %refs_2_.1, bf16[1,1,32,128]{3,2,1,0:T(8,128)(2,1)} %refs_3_.1, bf16[1,1,16,128]{3,2,1,0:T(8,128)(2,1)} %refs_4_.1, ...), custom_call_target="tpu_custom_call" | custom-call | tf_op jit(solution)/shard_map/solve/pallas_call | solution.py:712
  182.6 1.7 hand_out.1

commit v3 on v2

--- a/solution.py
+++ b/solution.py
@@ -97,13 +97,12 @@
     t.g = per(lambda h: vm(16, 128, 128) if h == 0 else vm(17, 64, 128), range(0, 4))
     t.g_send = per(lambda h: dma(()), range(0, 4))
     t.g_recv = per(lambda h: dma((16,)), range(0, 4))
-    t.x_out = per(lambda h: vm(2, 16, 64, 128), high)
-    t.x_in = per(lambda h: vm(15, 2, 64, 128), high)
+    t.x_out = per(lambda h: vm(2, 16, 64, 128) if h == 1 else vm(16, 256 >> h, 128), high)
+    t.x_in = per(lambda h: vm(15, 2, 64, 128) if h == 1 else vm(15, 256 >> h, 128), high)
     t.x_send = per(lambda h: dma(()), high)
     t.x_recv = per(lambda h: dma(()), high)
-    t.x_sum = per(lambda h: vm(2, 64, 128, dtype=F32), high)
-    t.x_full = per(lambda h: vm(2, 64, 128, dtype=F32), high)
-    t.x_rows = per(lambda h: vm(128, 128, dtype=F32), high)
+    t.x_sum = per(lambda h: vm(2, 64, 128, dtype=F32) if h == 1 else vm(256 >> h, 128, dtype=F32), high)
+    t.x_full = per(lambda h: vm(2, 64, 128, dtype=F32) if h == 1 else vm(256 >> h, 128, dtype=F32), high)
     t.xx = per(lambda h: dma((2,)), high)
     t.x0_out = vm(16, 2, 128, 128)
     t.x0_in = vm(16, 2, 128, 128)
@@ -508,18 +507,26 @@
 
     def take_x(h):
         wait(s.x_in[h], s.x_recv[h])
-        n = 2 ** (h - 1)
-        s.x_sum[h][...] = summed(s.x_in[h], s.x_out[h][:, f // n].astype(F32))
-        s.x_full[h][c] = s.x_sum[h][c]
-        remote(s.x_sum[h].at[other], s.x_full[h].at[c], s.xx[h].at[0], s.xx[h].at[1],
-               dev(z, other, f)).start()
+        if h == 1:
+            s.x_sum[1][...] = summed(s.x_in[1], s.x_out[1][:, f].astype(F32))
+            s.x_full[1][c] = s.x_sum[1][c]
+            src, dst = s.x_sum[1].at[other], s.x_full[1].at[c]
+        else:
+            s.x_sum[h][...] = summed(s.x_in[h], s.x_out[h][f].astype(F32))
+            src, dst = s.x_sum[h], s.x_full[h]
+        remote(src, dst, s.xx[h].at[0], s.xx[h].at[1], dev(z, other, f)).start()
 
     def give_x(h):
-        wait(s.x_full[h].at[0], s.xx[h].at[1])
-        n = 2 ** (h - 1)
         m = 256 >> h
-        s.x_rows[h][...] = s.x_full[h][...].reshape(128, 128).T
-        out[m:2 * m, :] = s.x_rows[h][rows((f % n) * m, m), :]
+        if h == 1:
+            wait(s.x_full[1].at[0], s.xx[1].at[1])
+            out[m:2 * m, :] = s.x_full[1][...].reshape(128, 128).T
+        else:
+            wait(s.x_full[h], s.xx[h].at[1])
+            theirs = s.x_full[h][...]
+            theirs = side_by_side([theirs[:, 64:], theirs[:, :64]])
+            lane = lax.broadcasted_iota(jnp.int32, (m, 128), 1)
+            out[m:2 * m, :] = jnp.where(lane // 64 == c, s.x_sum[h][...], theirs)
 
     def reaction(h):
         def pair(ks):
@@ -539,19 +546,33 @@
         return acc + pair([f, source(0)])
 
     def send_rows(h):
-        n, zrel, _ = group(h)
+        _, zrel, _ = group(h)
         half = 32 >> h
-        for part in range(2):
-            def x_step(q, part=part):
-                both = dot(s.w[h][...], columns(s.v[h], zrel * 2 * half + part * half + 2 * q, 2),
-                           NN).astype(BF)
-                s.x_out[h][part, 2 * q] = both[:, :128]
-                s.x_out[h][part, 2 * q + 1] = both[:, 128:]
-
-            loop(0, half // 2, x_step)
-
-        loop(0, 15, lambda k: remote(s.x_out[h].at[:, plane(k) // n], s.x_in[h].at[k], s.x_send[h],
-                                     s.x_recv[h], dev(z, c, plane(k))).start())
+        first = zrel * 2 * half
+        w = s.w[h][...]
+        if h == 1:
+            for part in range(2):
+                def x_step(q, part=part):
+                    both = dot(w, columns(s.v[1], first + part * half + 2 * q, 2), NN).astype(BF)
+                    s.x_out[1][part, 2 * q] = both[:, :128]
+                    s.x_out[1][part, 2 * q + 1] = both[:, 128:]
+
+                loop(0, half // 2, x_step)
+        else:
+            m = 256 >> h
+
+            def row_step(q):
+                both = [dot(w, columns(s.v[h], first + part * half + q), NN) for part in range(2)]
+                turned = jnp.concatenate(both, axis=0).T.astype(BF)
+                s.x_out[h][pl.ds(q * (128 // m), 128 // m)] = turned.reshape(128 // m, m, 128)
+
+            loop(0, half, row_step)
+
+        def send(k):
+            src = s.x_out[1].at[:, plane(k)] if h == 1 else s.x_out[h].at[plane(k)]
+            remote(src, s.x_in[h].at[k], s.x_send[h], s.x_recv[h], dev(z, c, plane(k))).start()
+
+        loop(0, 15, send)
 
     def send_g(h):
         at = s.g[h].at[f]
@@ -592,8 +613,6 @@
         by_fours(down)
 
         if h < 4:
-            send_rows(h)
-        if h < 4:
             take_x(h + 1)
 
         wait(s.sel_in[h], s.sel_recv[h])
@@ -616,6 +635,7 @@
             wait(half, s.g_swap.at[1])
         send_g(h - 1)
         if h < 4:
+            send_rows(h)
             give_x(h + 1)
         else:
             wait(s.yz[4].at[pl.ds(1, 3)], s.yz_recv[4])
@@ -689,7 +709,7 @@
             wait(s.yz[h].at[pl.ds(1, 64 // SHARE[h] - 1)], s.yz_send[h])
         wait(s.vb[h].at[:, pl.ds(0, 15)], s.vb_send[h])
         wait(s.x_in[h], s.x_send[h])
-        wait(s.x_sum[h].at[0], s.xx[h].at[0])
+        wait(s.x_sum[1].at[0] if h == 1 else s.x_sum[h], s.xx[h].at[0])
         if h < 4:
             wait(s.up_in[h], s.up_send[h])
             wait(s.g[h].at[pl.ds(0, 15)], s.g_send[h])

time: 184 us -> 173 us (0.940)
  Pallas kernels: 184 us -> 172 us
    pallas_call x1, Pallas kernels: 182 us -> 171 us  [on_device(): pl.pallas_call(kernel, out_shape=jax.ShapeDtypeStruct((512, 128), F32), i...]
where the time goes in v3:
time: 173 us
  Pallas kernels  172 us (99%)
    pallas_call x1, Pallas kernels, on_device(): pl.pallas_call(kernel, out_shape=jax.ShapeDtypeStruct((512, 128), F32), i...  171 us

profile of v3, /device:TPU:1, one launch (start us, length us, event | category | flops | bytes accessed | tf_op | source)
XLA Modules:
  0.0 173.0 jit_solution(12044905868631176155)
XLA Ops:
  0.6 170.7 %solve.1.packed_rows = f32[512,128]{1,0:T(8,128)} custom-call(bf16[1,1,256,128]{3,2,1,0:T(8,128)(2,1)} %refs_0_.1, bf16[1,1,128,128]{3,2,1,0:T(8,128)(2,1)} %refs_1_.1, bf16[1,1,64,128]{3,2,1,0:T(8,128)(2,1)} %refs_2_.1, bf16[1,1,32,128]{3,2,1,0:T(8,128)(2,1)} %refs_3_.1, bf16[1,1,16,128]{3,2,1,0:T(8,128)(2,1)} %refs_4_.1, ...), custom_call_target="tpu_custom_call" | custom-call | tf_op jit(solution)/shard_map/solve/pallas_call | solution.py:732
  171.4 1.7 hand_out.1

commit v4 on v3

--- a/solution.py
+++ b/solution.py
@@ -671,10 +671,10 @@
         wait(s.x0_in.at[k], s.x0_recv.at[k])
         s.x0_sum[...] = s.x0_sum[...] + s.x0_in[k].astype(F32)
 
+    give_x(1)
     loop(f + 1, FRONT, x0_take)
     for k in range(2):
         out[256 + k * 128:256 + (k + 1) * 128, :] = s.x0_sum[k].T
-    give_x(1)
 
     loop(0, f, lambda k: wait(s.x0_out.at[k], s.x0_send.at[k]))
     loop(f + 1, FRONT, lambda k: wait(s.r.at[pl.ds(0, 2)], s.r_send.at[k]))

time: 173 us -> 173 us (level)
  no operation moved by 1% of the time
where the time goes in v4:
time: 173 us
  Pallas kernels  172 us (99%)
    pallas_call x1, Pallas kernels, on_device(): pl.pallas_call(kernel, out_shape=jax.ShapeDtypeStruct((512, 128), F32), i...  171 us

profile of v4, /device:TPU:1, one launch (start us, length us, event | category | flops | bytes accessed | tf_op | source)
XLA Modules:
  0.0 173.0 jit_solution(14102279896233127514)
XLA Ops:
  0.6 170.6 %solve.1.packed_rows = f32[512,128]{1,0:T(8,128)} custom-call(bf16[1,1,256,128]{3,2,1,0:T(8,128)(2,1)} %refs_0_.1, bf16[1,1,128,128]{3,2,1,0:T(8,128)(2,1)} %refs_1_.1, bf16[1,1,64,128]{3,2,1,0:T(8,128)(2,1)} %refs_2_.1, bf16[1,1,32,128]{3,2,1,0:T(8,128)(2,1)} %refs_3_.1, bf16[1,1,16,128]{3,2,1,0:T(8,128)(2,1)} %refs_4_.1, ...), custom_call_target="tpu_custom_call" | custom-call | tf_op jit(solution)/shard_map/solve/pallas_call | solution.py:732
  171.3 1.7 hand_out.1
